TPU v7x, 256 devices: a whole 4x4x8 slice. The times are simulated.
256 devices in a mesh: attn: 16 (over y_lo, x, core), ffn: 8 (over z), grp: 2 (over y_hi).
Axes of the slice: x: 4, y: 4 (y_hi: 2, y_lo: 2; y = y_hi * 2 + y_lo), z: 8, core: 2. Of those that a mesh axis runs over, the one named last changes fastest.
Arguments:
- query: bfloat16 [2048, 8192], P(('grp', 'attn'), 'ffn'), parts along dimension 0, may hold values from -5 to 5
- key_store_cache: bfloat16 [2048, 192, 1024], P(('grp', 'attn'), None, 'ffn'), parts along dimension 0, may hold values from -5 to 5
- value_store_cache: bfloat16 [2048, 192, 1024], P(('grp', 'attn'), None, 'ffn'), parts along dimension 0, may hold values from -5 to 5
- token_keys: bfloat16 [2048, 1024], P(('grp', 'attn'), 'ffn'), parts along dimension 0, may hold values from -5 to 5
- token_values: bfloat16 [2048, 1024], P(('grp', 'attn'), 'ffn'), parts along dimension 0, may hold values from -5 to 5
- pooled_block_keys: bfloat16 [512, 16, 1024], P(('grp', 'attn'), None, 'ffn'), parts along dimension 0, may hold values from -5 to 5
- pooled_block_values: bfloat16 [512, 16, 1024], P(('grp', 'attn'), None, 'ffn'), parts along dimension 0, may hold values from -6 to 6
- block_dst: int32 [512, 1], P('grp'), parts along dimension 0, may hold values from 0 to 15; in each aligned block of 16 rows (0 to 15, 16 to 31, ...) at most 2 rows name the same one
- block_row: int32 [512], P('grp'), parts along dimension 0, may hold values from 0 to 63
- ctx_len: int32 [2048], P(('grp', 'attn')), parts along dimension 0, may hold values from 1 to 192, as said below
- residual: bfloat16 [2048, 8192], P('grp', 'attn'), parts along dimension 0, may hold values from -15 to 15
- norm_gain: float32 [8192], P('attn'), may hold values from 0.1 to 1.9
- output_weight: bfloat16 [8192, 8192], P('ffn', 'attn'), may hold values from -0.1875 to 0.1875
- w_gate: bfloat16 [8192, 14336], P('attn', 'ffn'), may hold values from -0.0625 to 0.0625
- w_up: bfloat16 [8192, 14336], P('attn', 'ffn'), may hold values from -0.0625 to 0.0625
- w_down: bfloat16 [14336, 8192], P('ffn', 'attn'), may hold values from -0.046875 to 0.046875
Outputs:
- layer_out: bfloat16 [2048, 8192], P(('grp', 'ffn'), 'attn'), parts along dimension 0
There are 2 independent parts, one for each index of `grp`. A program takes and returns all parts, laid end to end along the dimension named above; an argument that names none is the same for every part. Nothing has to cross between parts.
Inputs may be any that keep to these rules, and one draw needn't show every extreme that they name: `block_dst`: of the 16 blocks held by one pool index (aligned blocks of rows), at most 2 name the same attention index. `ctx_len`: every attention index holds a request that uses all 192 cached positions.
All inputs are finite; a program needn't handle non-finite values.
Results may differ from a plain program's by a relative error of at most 0.024.
Values may be sent and summed in bfloat16 or wider, within the bound.
No kernel may reach another device: no remote copies, remote signals or barrier semaphores. Data moves between devices by JAX's collectives and lax.ppermute only.
A program may use at most 128 MiB of HBM per device.

v0:
```python
import jax
import jax.numpy as jnp
from jax import lax
from jax.sharding import PartitionSpec as P

MODEL_WIDTH = 8192
QUERY_HEADS = 64
KEY_VALUE_HEADS = 8
HEAD_SIZE = 128
CAP = 2


epsilon = 1e-05


def body(
    query,
    key_store_cache,
    value_store_cache,
    token_keys,
    token_values,
    pooled_block_keys,
    pooled_block_values,
    block_dst,
    block_row,
    ctx_len,
    residual,
    norm_gain,
    output_weight,
    w_gate,
    w_up,
    w_down,
):
    tok_rows = query.shape[0]
    ctx_size = key_store_cache.shape[1]
    head_width = key_store_cache.shape[2]
    groups = head_width // HEAD_SIZE
    group_rows = QUERY_HEADS // KEY_VALUE_HEADS
    block_len = pooled_block_keys.shape[1]
    local_pool = pooled_block_keys.shape[0]
    attn_size = lax.axis_size("attn")
    my_index = lax.axis_index("attn")
    slot_count = attn_size * CAP
    dst_table = block_dst[:, 0].reshape(attn_size, local_pool)
    row_table = block_row.reshape(attn_size, local_pool)
    positions = jnp.arange(local_pool, dtype=jnp.int32)
    earlier = positions[None, :] < positions[:, None]
    same_dst = dst_table[:, :, None] == dst_table[:, None, :]
    rank_table = jnp.sum((same_dst & earlier[None]).astype(jnp.int32), axis=2)
    own_dst = lax.dynamic_index_in_dim(dst_table, my_index, 0, keepdims=False)
    own_rank = lax.dynamic_index_in_dim(rank_table, my_index, 0, keepdims=False)
    slot_index = own_dst * CAP + own_rank
    picker = (jnp.arange(slot_count, dtype=jnp.int32)[:, None] == slot_index[None, :]).astype(
        jnp.bfloat16
    )
    flat_keys = pooled_block_keys.reshape(local_pool, block_len * head_width)
    flat_values = pooled_block_values.reshape(local_pool, block_len * head_width)
    send_keys = (
        jnp.dot(picker, flat_keys, preferred_element_type=jnp.float32)
        .astype(jnp.bfloat16)
        .reshape(slot_count, block_len, head_width)
    )
    send_values = (
        jnp.dot(picker, flat_values, preferred_element_type=jnp.float32)
        .astype(jnp.bfloat16)
        .reshape(slot_count, block_len, head_width)
    )
    recv_keys, recv_values = (
        lax.all_to_all(send_keys, "attn", split_axis=0, concat_axis=0, tiled=True),
        lax.all_to_all(send_values, "attn", split_axis=0, concat_axis=0, tiled=True),
    )
    cap_slots = jnp.arange(CAP, dtype=jnp.int32)
    hit_mask = (dst_table == my_index)[:, None, :] & (
        rank_table[:, None, :] == cap_slots[None, :, None]
    )
    recv_row = (jnp.sum(jnp.where(hit_mask, row_table[:, None, :] + 1, 0), axis=2) - 1).reshape(
        slot_count
    )
    score_scale = HEAD_SIZE ** (-0.5)
    query_rows = query.reshape(tok_rows, groups, group_rows, HEAD_SIZE)
    stored_keys = key_store_cache.reshape(tok_rows, ctx_size, groups, HEAD_SIZE)
    stored_values = value_store_cache.reshape(tok_rows, ctx_size, groups, HEAD_SIZE)
    score_cache = (
        jnp.einsum("bghd,btgd->bght", query_rows, stored_keys, preferred_element_type=jnp.float32)
        * score_scale
    )
    valid_mask = jnp.arange(ctx_size, dtype=jnp.int32)[None, :] < ctx_len[:, None]
    score_cache = jnp.where(valid_mask[:, None, None, :], score_cache, -jnp.inf)
    resumed_keys = recv_keys.reshape(slot_count * block_len, groups, HEAD_SIZE)
    resumed_values = recv_values.reshape(slot_count * block_len, groups, HEAD_SIZE)
    score_recv = (
        jnp.einsum("bghd,tgd->bght", query_rows, resumed_keys, preferred_element_type=jnp.float32)
        * score_scale
    )
    owner_mask = (
        jnp.repeat(recv_row, block_len)[None, :] == jnp.arange(tok_rows, dtype=jnp.int32)[:, None]
    )
    score_recv = jnp.where(owner_mask[:, None, None, :], score_recv, -jnp.inf)
    current_keys = token_keys.reshape(tok_rows, groups, HEAD_SIZE)
    score_new = (
        jnp.einsum("bghd,bgd->bgh", query_rows, current_keys, preferred_element_type=jnp.float32)
        * score_scale
    )
    row_max = jnp.maximum(
        jnp.maximum(jnp.max(score_cache, axis=-1), jnp.max(score_recv, axis=-1)), score_new
    )
    exp_cache = jnp.exp(score_cache - row_max[..., None])
    exp_recv = jnp.exp(score_recv - row_max[..., None])
    exp_new = jnp.exp(score_new - row_max)
    denominator = jnp.sum(exp_cache, axis=-1) + jnp.sum(exp_recv, axis=-1) + exp_new
    prob_cache = (exp_cache / denominator[..., None]).astype(jnp.bfloat16)
    prob_recv = (exp_recv / denominator[..., None]).astype(jnp.bfloat16)
    prob_new = (exp_new / denominator).astype(jnp.bfloat16)
    weighted = jnp.einsum(
        "bght,btgd->bghd", prob_cache, stored_values, preferred_element_type=jnp.float32
    )
    weighted = weighted + jnp.einsum(
        "bght,tgd->bghd", prob_recv, resumed_values, preferred_element_type=jnp.float32
    )
    current_values = token_values.reshape(tok_rows, groups, HEAD_SIZE).astype(jnp.float32)
    weighted = weighted + prob_new.astype(jnp.float32)[..., None] * current_values[:, :, None, :]
    attended = weighted.reshape(tok_rows, groups * group_rows * HEAD_SIZE).astype(jnp.bfloat16)
    head_part = jnp.dot(
        lax.all_gather(attended, "attn", axis=0, tiled=True),
        output_weight,
        preferred_element_type=jnp.float32,
    )
    ffn_size = lax.axis_size("ffn")
    ffn_index = lax.axis_index("ffn")
    share_rows = head_part.shape[0] // ffn_size
    attn_out = lax.psum(head_part.astype(jnp.bfloat16), "ffn").astype(jnp.float32)
    mixed = residual.astype(jnp.float32) + attn_out
    squares = lax.psum(jnp.sum(mixed * mixed, axis=1), "attn")
    normed = (mixed * lax.rsqrt(squares / MODEL_WIDTH + epsilon)[:, None] * norm_gain).astype(
        jnp.bfloat16
    )
    kept_rows = lax.dynamic_slice_in_dim(mixed, ffn_index * share_rows, share_rows, 0)
    hidden_width = w_gate.shape[1]
    gate_up = lax.psum_scatter(
        jnp.concatenate(
            [
                jnp.dot(normed, w_gate, preferred_element_type=jnp.float32),
                jnp.dot(normed, w_up, preferred_element_type=jnp.float32),
            ],
            axis=1,
        ).astype(jnp.bfloat16),
        "attn",
        scatter_dimension=0,
        tiled=True,
    ).astype(jnp.float32)
    activated = (jax.nn.silu(gate_up[:, :hidden_width]) * gate_up[:, hidden_width:]).astype(
        jnp.bfloat16
    )
    down_part = jnp.dot(
        lax.all_gather(activated, "attn", axis=0, tiled=True),
        w_down,
        preferred_element_type=jnp.float32,
    )
    ffn_share = lax.psum_scatter(
        down_part.astype(jnp.bfloat16), "ffn", scatter_dimension=0, tiled=True
    ).astype(jnp.float32)
    return (kept_rows + ffn_share).astype(jnp.bfloat16)


def solution(mesh):
    placed = (
        P(("grp", "attn"), "ffn"),
        P(("grp", "attn"), None, "ffn"),
        P(("grp", "attn"), None, "ffn"),
        P(("grp", "attn"), "ffn"),
        P(("grp", "attn"), "ffn"),
        P(("grp", "attn"), None, "ffn"),
        P(("grp", "attn"), None, "ffn"),
        P("grp", None),
        P("grp"),
        P(("grp", "attn")),
        P("grp", "attn"),
        P("attn"),
        P("ffn", "attn"),
        P("attn", "ffn"),
        P("attn", "ffn"),
        P("ffn", "attn"),
    )
    return jax.shard_map(
        body, mesh=mesh, in_specs=placed, out_specs=P(("grp", "ffn"), "attn"), check_vma=False
    )
```

profile of v0, /device:TPU:2, one launch (start us, length us, event | category | flops | bytes accessed | tf_op | source)
XLA Modules:
  0.0 378.0 jit_solution(17119664770401599803)
XLA Ops:
  7.1 1.6 reduce.9
  9.2 1.0 fusion.6
  10.9 5.9 %all-to-all-start = ((bf16[32,16,128]{2,1,0:T(8,128)(2,1)}), bf16[32,16,128]{2,1,0:T(8,128)(2,1)S(1)}, u32[]{:S(2)}, u32[]{:S(2)}) async-start(bf16[32,16,128]{2,1,0:T(8,128)(2,1)} %bitcast.24), calls=%async_computation | async-start | bytes 262144 | tf_op jit(solution)/shard_map/all_to_all | solution.py:69
  18.6 0.7 iota_compare_fusion.1
  19.3 1.3 convert_element_type.71
  20.6 1.0 fusion.7
  22.3 0.9 copy.56
  23.2 0.9 fusion.21
  24.8 3.2 fusion.30
  28.0 0.8 copy.45
  29.5 5.7 %all-to-all-start.1 = ((bf16[32,16,128]{2,1,0:T(8,128)(2,1)}), bf16[32,16,128]{2,1,0:T(8,128)(2,1)}, u32[]{:S(2)}, u32[]{:S(2)}) async-start(bf16[32,16,128]{2,1,0:T(8,128)(2,1)} %bitcast.28), calls=%async_computation.1 | async-start | bytes 262144 | tf_op jit(solution)/shard_map/all_to_all | solution.py:70
  35.3 1.3 fusion.31
  37.4 1.5 fusion.8
  38.9 1.3 fusion.11
  40.4 3.1 convolution_bitcast_fusion.1
  43.5 1.1 fusion.10
  44.7 1.5 fusion.5
  47.0 38.8 %all-gather.3.cloned.1.call-done = bf16[1024,1024]{1,0:T(8,128)(2,1)} async-done(((bf16[64,1024]{1,0:T(8,128)(2,1)}), bf16[1024,1024]{1,0:T(8,128)(2,1)}) %all-gather.3.cloned.1.call-update) | async-done | bytes 2097168 | tf_op jit(solution)/shard_map/all_gather | solution.py:124
  85.8 4.1 %convolution_convert_fusion.4 = bf16[1024,512]{1,0:T(8,128)(2,1)} fusion(bf16[1024,1024]{1,0:T(8,128)(2,1)} %all-gather.3.cloned.1.call-done, bf16[1024,512]{1,0:T(8,128)(2,1)} %param.28), kind=kOutput, calls=%fused_computation.8 | convolution fusion | flops 1074266112 | bytes 4194304 | tf_op jit(solution)/shard_map/dot_general | solution.py:123
  90.0 76.5 %all-reduce.2.cloned.1.call-done = bf16[1024,512]{1,0:T(8,128)(2,1)} async-done(((bf16[1024,512]{1,0:T(8,128)(2,1)}), bf16[1024,512]{1,0:T(8,128)(2,1)}) %all-reduce.2.cloned.1.call-update) | async-done | bytes 1048592 | tf_op jit(solution)/shard_map/psum | solution.py:131
  166.5 3.2 convert_add_fusion
  169.7 23.6 %psum.15 = f32[1024]{0:T(1024)S(1)} all-reduce(f32[1024]{0:T(1024)S(1)} %get-tuple-element.8), channel_id=1, replica_groups=mesh['attn'=16,'ffn'=8,'grp'=2] {'attn'}, use_global_device_ids=true, to_apply=%region_8.9 | all-reduce | flops 1024 | bytes 8192 | tf_op jit(solution)/shard_map/psum | solution.py:133
  193.4 6.4 %convolution_convert_fusion = bf16[1024,1792]{1,0:T(8,128)(2,1)} fusion(bf16[512,1792]{1,0:T(8,128)(2,1)} %param.30, f32[512]{0:T(512)S(1)} %copy-done.8, f32[1024]{0:T(1024)S(1)} %add_rsqrt_fusion, bf16[1024,512]{1,0:T(8,128)(2,1)} %all-reduce.2.cloned.1.call-done, bf16[1024,512]{1,0:T(8,128)(2,1)} %param.26), kind=kOutput, calls=%fused_computation.1 | convolution fusion | flops 1884028928 | bytes 7608320 | tf_op jit(solution)/shard_map/dot_general | solution.py:143
  199.8 4.2 %convolution_convert_fusion.1 = bf16[1024,1792]{1,0:T(8,128)(2,1)} fusion(bf16[512,1792]{1,0:T(8,128)(2,1)S(1)} %copy-done.7, f32[512]{0:T(512)S(1)} %copy-done.8, f32[1024]{0:T(1024)S(1)} %add_rsqrt_fusion, bf16[1024,512]{1,0:T(8,128)(2,1)S(1)} %copy-done.3, bf16[1024,512]{1,0:T(8,128)(2,1)S(1)} %copy-done.2), kind=kOutput, calls=%fused_computation.2 | convolution fusion | flops 1884028928 | bytes 7608320 | tf_op jit(solution)/shard_map/dot_general | solution.py:142
  204.0 6.6 %pad_maximum_fusion = bf16[1024,3584]{1,0:T(8,128)(2,1)} fusion(bf16[1024,1792]{1,0:T(8,128)(2,1)} %convolution_convert_fusion, bf16[1024,1792]{1,0:T(8,128)(2,1)} %convolution_convert_fusion.1), kind=kLoop, calls=%fused_computation | loop fusion | flops 14680064 | bytes 14680064 | tf_op jit(solution)/shard_map/concatenate | solution.py:140
  210.7 70.3 %reduce-scatter.3.cloned.1.call-done = bf16[64,3584]{1,0:T(8,128)(2,1)} async-done(((bf16[1024,3584]{1,0:T(8,128)(2,1)}), bf16[64,3584]{1,0:T(8,128)(2,1)}) %reduce-scatter.3.cloned.1.call-update) | async-done | bytes 458768 | tf_op jit(solution)/shard_map/reduce_scatter | solution.py:139
  281.0 1.1 convert_element_type.77
  282.1 0.8 fusion.12
  283.0 42.0 %all-gather.5.cloned.1.call-done = bf16[1024,1792]{1,0:T(8,128)(2,1)} async-done(((bf16[64,1792]{1,0:T(8,128)(2,1)}), bf16[1024,1792]{1,0:T(8,128)(2,1)}) %all-gather.5.cloned.1.call-update) | async-done | bytes 3670032 | tf_op jit(solution)/shard_map/all_gather | solution.py:155
  325.0 5.6 %convolution_convert_fusion.5 = bf16[1024,512]{1,0:T(8,128)(2,1)} fusion(bf16[1024,1792]{1,0:T(8,128)(2,1)} %all-gather.5.cloned.1.call-done, bf16[1792,512]{1,0:T(8,128)(2,1)} %param.31), kind=kOutput, calls=%fused_computation.9 | convolution fusion | flops 1879572480 | bytes 6553600 | tf_op jit(solution)/shard_map/dot_general | solution.py:154
  330.6 39.2 %reduce-scatter.5.cloned.1.call-done = bf16[128,512]{1,0:T(8,128)(2,1)} async-done(((bf16[1024,512]{1,0:T(8,128)(2,1)}), bf16[128,512]{1,0:T(8,128)(2,1)}) %reduce-scatter.5.cloned.1.call-update) | async-done | bytes 131088 | tf_op jit(solution)/shard_map/reduce_scatter | solution.py:159
  369.8 1.7 add_convert_fusion
  (56 shorter events, 7.6 us)
Async XLA Ops:
  6.5 18.3 %copy-start = (bf16[64,192,128]{2,1,0:T(8,128)(2,1)S(1)}, bf16[64,192,128]{2,1,0:T(8,128)(2,1)}, u32[]{:S(2)}) copy-start(bf16[64,192,128]{2,1,0:T(8,128)(2,1)} %param.17) | copy-start | bytes 9437188
  10.9 18.6 %all-to-all-start = ((bf16[32,16,128]{2,1,0:T(8,128)(2,1)}), bf16[32,16,128]{2,1,0:T(8,128)(2,1)S(1)}, u32[]{:S(2)}, u32[]{:S(2)}) async-start(bf16[32,16,128]{2,1,0:T(8,128)(2,1)} %bitcast.24), calls=%async_computation | async-start | bytes 262144 | tf_op jit(solution)/shard_map/all_to_all | solution.py:69
  24.8 10.5 %copy-start.4 = (bf16[64,1024]{1,0:T(8,128)(2,1)S(1)}, bf16[64,1024]{1,0:T(8,128)(2,1)}, u32[]{:S(2)}) copy-start(bf16[64,1024]{1,0:T(8,128)(2,1)} %param.16) | copy-start | bytes 393220
  28.0 12.3 %copy-start.5 = (f32[64,1,8]{0,2,1:T(8,128)S(1)}, f32[64,1,8]{0,2,1:T(8,128)}, u32[]{:S(2)}) copy-start(f32[64,1,8]{0,2,1:T(8,128)} %copy.52) | copy-start | bytes 6148
  29.5 15.1 %all-to-all-start.1 = ((bf16[32,16,128]{2,1,0:T(8,128)(2,1)}), bf16[32,16,128]{2,1,0:T(8,128)(2,1)}, u32[]{:S(2)}, u32[]{:S(2)}) async-start(bf16[32,16,128]{2,1,0:T(8,128)(2,1)} %bitcast.28), calls=%async_computation.1 | async-start | bytes 262144 | tf_op jit(solution)/shard_map/all_to_all | solution.py:70
  35.3 50.5 %all-gather.3.cloned.1.call-start = ((), (), s32[]{:S(2)}) async-start(), calls=%async_computation.4 | async-start | bytes 2228224 | tf_op jit(solution)/shard_map/all_gather | solution.py:124
  40.4 3.1 copy-start.1
  40.4 4.3 %copy-start.6 = (f32[64,128]{1,0:T(8,128)S(1)}, f32[64,128]{1,0:T(8,128)}, u32[]{:S(2)}) copy-start(f32[64,128]{1,0:T(8,128)} %convert_element_type.71) | copy-start | bytes 98308
  46.9 119.6 %all-reduce.2.cloned.1.call-start = ((), (), s32[]{:S(2)}) async-start(), calls=%async_computation.5 | async-start | bytes 2097152 | tf_op jit(solution)/shard_map/psum | solution.py:131
  89.9 103.4 %copy-start.8 = (f32[512]{0:T(512)S(1)}, f32[512]{0:T(512)}, u32[]{:S(2)}) copy-start(f32[512]{0:T(512)} %param.27) | copy-start | bytes 6148
  89.9 191.1 %reduce-scatter.3.cloned.1.call-start = ((), (), s32[]{:S(2)}) async-start(), calls=%async_computation.6 | async-start | bytes 7798784 | tf_op jit(solution)/shard_map/reduce_scatter | solution.py:139
  193.3 6.4 %copy-start.2 = (bf16[1024,512]{1,0:T(8,128)(2,1)S(1)}, bf16[1024,512]{1,0:T(8,128)(2,1)}, u32[]{:S(2)}) copy-start(bf16[1024,512]{1,0:T(8,128)(2,1)} %param.26) | copy-start | bytes 3145732
  193.4 6.4 %copy-start.3 = (bf16[1024,512]{1,0:T(8,128)(2,1)S(1)}, bf16[1024,512]{1,0:T(8,128)(2,1)}, u32[]{:S(2)}) copy-start(bf16[1024,512]{1,0:T(8,128)(2,1)} %all-reduce.2.cloned.1.call-done) | copy-start | bytes 3145732
  193.4 6.4 %copy-start.7 = (bf16[512,1792]{1,0:T(8,128)(2,1)S(1)}, bf16[512,1792]{1,0:T(8,128)(2,1)}, u32[]{:S(2)}) copy-start(bf16[512,1792]{1,0:T(8,128)(2,1)} %param.29) | copy-start | bytes 5505028
  210.6 114.3 %all-gather.5.cloned.1.call-start = ((), (), s32[]{:S(2)}) async-start(), calls=%async_computation.7 | async-start | bytes 3899392 | tf_op jit(solution)/shard_map/all_gather | solution.py:155
  282.9 86.8 %reduce-scatter.5.cloned.1.call-start = ((), (), s32[]{:S(2)}) async-start(), calls=%async_computation.8 | async-start | bytes 1179648 | tf_op jit(solution)/shard_map/reduce_scatter | solution.py:159
Sparse Core Ops, SparseCore 0:
  47.0 38.7 all-gather.2
  90.0 76.4 all-reduce.1
  210.8 70.1 reduce-scatter.2
  283.0 41.8 all-gather.4
  330.7 38.9 reduce-scatter.4
where the time goes:
time: 379 us; the launch traced here: 378 us
  waiting for transfers between devices  267 us (70%)
  matrix products  32.3 us (9%)
  other arithmetic  23.7 us (6%)
  blocking collectives  23.6 us (6%)
  between operations  13.3 us (4%)
  starting transfers between devices  11.8 us (3%)
  local copies, waits for them, and re-layouts  6.4 us (2%)
    psum x1, waiting for transfers between devices, body(): lax.psum(head_part.astype(jnp.bfloat16), 'ffn').astype(jnp.float32)  76.5 us
    reduce_scatter x1, waiting for transfers between devices, body(): lax.psum_scatter(jnp.concatenate([jnp.dot(normed, w_gate, preferred_eleme...  70.3 us
    all_gather x1, waiting for transfers between devices, body(): lax.all_gather(activated, 'attn', axis=0, tiled=True)  42 us
    reduce_scatter x1, waiting for transfers between devices, body(): lax.psum_scatter(down_part.astype(jnp.bfloat16), 'ffn', scatter_dimension...  39.2 us
    all_gather x1, waiting for transfers between devices, body(): lax.all_gather(attended, 'attn', axis=0, tiled=True)  38.8 us
    psum x1, blocking collectives, body(): squares = lax.psum(jnp.sum(mixed * mixed, axis=1), 'attn')  23.6 us
  transfers between devices with their start and end apart: 7, of which 5 were waited for; matrix products, arithmetic and copies ran while one was open for 6% of the time, Pallas kernels for 0%

commit v1 on v0

v1 whole, which is shorter than its diff:
```python
import jax
import jax.numpy as jnp
from jax import lax
from jax.experimental import pallas as pl
from jax.experimental.pallas import tpu as pltpu
from jax.sharding import PartitionSpec as P

MODEL_WIDTH = 8192
HEAD_SIZE = 128
HEADS = 8
CAP = 2
CHIPS = 8
epsilon = 1e-05
BF = jnp.bfloat16
F32 = jnp.float32
VMEM_BYTES = 40 * 1024 * 1024
NT = (((1,), (1,)), ((), ()))


def params():
    return pltpu.CompilerParams(vmem_limit_bytes=VMEM_BYTES)


def whole(shape):
    return pl.BlockSpec(shape, lambda *_: (0,) * len(shape))


def cost(flops, size):
    return pl.CostEstimate(flops=flops, bytes_accessed=size, transcendentals=0)


def swap_core(value):
    return lax.ppermute(value, "attn", [(a, a ^ 1) for a in range(16)])


def exchange_chips(value):
    groups = [[2 * k + c for k in range(CHIPS)] for c in range(2)]
    return lax.all_to_all(
        value, "attn", split_axis=0, concat_axis=0, axis_index_groups=groups, tiled=True
    )


def z_shift(value, step):
    return lax.ppermute(value, "ffn", [(f, (f + step) % 8) for f in range(8)])


def z_scatter_sum(take):
    right, left = take(4), take(-3)
    for step in range(1, 5):
        right = z_shift(right, 1)
        if step < 4:
            right = (right.astype(F32) + take(4 - step).astype(F32)).astype(BF)
            left = z_shift(left, -1)
            if step < 3:
                left = (left.astype(F32) + take(step - 3).astype(F32)).astype(BF)
    return right.astype(F32) + left.astype(F32) + take(0).astype(F32)


def z_gather(value):
    right = left = value
    blocks = [None] * 8
    blocks[0] = value
    for step in range(1, 5):
        right = z_shift(right, 1)
        blocks[8 - step] = right
        if step < 4:
            left = z_shift(left, -1)
            blocks[step] = left
    return blocks


def place_blocks(block_dst, pooled_keys, pooled_values):
    held, block_len, width = pooled_keys.shape
    slots = 16 * CAP

    def kernel(dst_ref, k_ref, v_ref, out_ref):
        first = lax.axis_index("attn") * held
        out_ref[...] = jnp.zeros_like(out_ref)
        dst = [dst_ref[first + j] for j in range(held)]
        for j in range(held):
            rank = jnp.int32(0)
            for i in range(j):
                rank = rank + jnp.where(dst[i] == dst[j], 1, 0)
            slot = dst[j] * CAP + jnp.minimum(rank, CAP - 1)
            out_ref[slot, :, :width] = k_ref[j]
            out_ref[slot, :, width:] = v_ref[j]

    return pl.pallas_call(
        kernel,
        out_shape=jax.ShapeDtypeStruct((slots, block_len, 2 * width), BF),
        in_specs=[
            pl.BlockSpec(memory_space=pltpu.SMEM),
            pl.BlockSpec(memory_space=pltpu.VMEM),
            pl.BlockSpec(memory_space=pltpu.VMEM),
        ],
        out_specs=pl.BlockSpec(memory_space=pltpu.VMEM),
        compiler_params=params(),
    )(block_dst, pooled_keys, pooled_values)


def attention(ctx_len, query, keys, values, token_keys, token_values, received, dst, rows):
    requests, ctx_size, width = keys.shape
    step_rows = 16
    slots = 16 * CAP
    block_len = received.shape[0] // slots
    recv_size = received.shape[0]
    scale = HEAD_SIZE**-0.5
    hrows = step_rows * HEADS

    def kernel(
        ctx_ref, q_ref, k_ref, v_ref, tk_ref, tv_ref, r_ref, dst_ref, row_ref,
        out_ref, owner_ref, q_buf, tk_buf, tv_buf, o_buf,
    ):
        step = pl.program_id(0)

        @pl.when(step == 0)
        def _():
            me = lax.axis_index("attn")
            hit = dst_ref[...] == me
            hit_f = hit.astype(F32)
            count = hit.shape[1]
            before = lax.broadcasted_iota(jnp.int32, (count, count), 0) < lax.broadcasted_iota(
                jnp.int32, (count, count), 1
            )
            rank = jnp.dot(hit_f, before.astype(F32), preferred_element_type=F32)
            marked = row_ref[...].astype(F32) + 1.0
            first = jnp.sum(jnp.where(hit & (rank < 0.5), marked, 0.0), axis=1, keepdims=True)
            second = jnp.sum(
                jnp.where(hit & (rank > 0.5) & (rank < 1.5), marked, 0.0), axis=1, keepdims=True
            )
            slot = lax.broadcasted_iota(jnp.int32, (16, recv_size), 1) // block_len
            pool = lax.broadcasted_iota(jnp.int32, (16, recv_size), 0)
            found = jnp.where(slot == pool * CAP, first, 0.0) + jnp.where(
                slot == pool * CAP + 1, second, 0.0
            )
            owner_ref[...] = jnp.broadcast_to(
                jnp.sum(found, axis=0, keepdims=True) - 1.0, owner_ref.shape
            )

        for h in range(HEADS):
            q_buf[pl.ds(h, step_rows, stride=HEADS), :] = q_ref[
                :, h * HEAD_SIZE : (h + 1) * HEAD_SIZE
            ].astype(F32)
            tk_buf[pl.ds(h, step_rows, stride=HEADS), :] = tk_ref[...].astype(F32)
            tv_buf[pl.ds(h, step_rows, stride=HEADS), :] = tv_ref[...].astype(F32)
        q_full = q_buf[...]
        q_half = q_full.astype(BF)
        scores = []
        spot = lax.broadcasted_iota(jnp.int32, (HEADS, ctx_size), 1)
        for b in range(step_rows):
            part = lax.dot_general(
                q_half[b * HEADS : (b + 1) * HEADS], k_ref[b], NT, preferred_element_type=F32
            )
            scores.append(
                jnp.where(spot < ctx_ref[step * step_rows + b], part * scale, -jnp.inf)
            )
        score_cache = jnp.concatenate(scores, axis=0)
        score_recv = (
            lax.dot_general(q_half, r_ref[:, :width], NT, preferred_element_type=F32) * scale
        )
        request = (
            lax.broadcasted_iota(jnp.int32, (hrows, recv_size), 0) // HEADS + step * step_rows
        )
        score_recv = jnp.where(request.astype(F32) == owner_ref[0:1, :], score_recv, -jnp.inf)
        score_new = jnp.sum(q_full * tk_buf[...], axis=1, keepdims=True) * scale
        top = jnp.maximum(
            jnp.maximum(
                jnp.max(score_cache, axis=1, keepdims=True),
                jnp.max(score_recv, axis=1, keepdims=True),
            ),
            score_new,
        )
        exp_cache = jnp.exp(score_cache - top)
        exp_recv = jnp.exp(score_recv - top)
        exp_new = jnp.exp(score_new - top)
        total = (
            jnp.sum(exp_cache, axis=1, keepdims=True)
            + jnp.sum(exp_recv, axis=1, keepdims=True)
            + exp_new
        )
        inverse = 1.0 / total
        prob_cache = (exp_cache * inverse).astype(BF)
        prob_recv = (exp_recv * inverse).astype(BF)
        prob_new = (exp_new * inverse).astype(BF).astype(F32)
        attended = [
            jnp.dot(
                prob_cache[b * HEADS : (b + 1) * HEADS], v_ref[b], preferred_element_type=F32
            )
            for b in range(step_rows)
        ]
        o_buf[...] = (
            jnp.concatenate(attended, axis=0)
            + jnp.dot(prob_recv, r_ref[:, width:], preferred_element_type=F32)
            + prob_new * tv_buf[...]
        )
        for h in range(HEADS):
            head = o_buf[pl.ds(h, step_rows, stride=HEADS), :].astype(BF)
            out_ref[:, :, h * HEAD_SIZE : (h + 1) * HEAD_SIZE] = jnp.broadcast_to(
                head[None], (CHIPS, step_rows, HEAD_SIZE)
            )

    return pl.pallas_call(
        kernel,
        grid=(requests // step_rows,),
        out_shape=jax.ShapeDtypeStruct((CHIPS, requests, query.shape[1]), BF),
        in_specs=[
            pl.BlockSpec(memory_space=pltpu.SMEM),
            pl.BlockSpec((step_rows, query.shape[1]), lambda i: (i, 0)),
            pl.BlockSpec((step_rows, ctx_size, width), lambda i: (i, 0, 0)),
            pl.BlockSpec((step_rows, ctx_size, width), lambda i: (i, 0, 0)),
            pl.BlockSpec((step_rows, width), lambda i: (i, 0)),
            pl.BlockSpec((step_rows, width), lambda i: (i, 0)),
            whole(received.shape),
            whole(dst.shape),
            whole(rows.shape),
        ],
        out_specs=pl.BlockSpec((CHIPS, step_rows, query.shape[1]), lambda i: (0, i, 0)),
        scratch_shapes=[
            pltpu.VMEM((8, recv_size), F32),
            pltpu.VMEM((hrows, HEAD_SIZE), F32),
            pltpu.VMEM((hrows, HEAD_SIZE), F32),
            pltpu.VMEM((hrows, HEAD_SIZE), F32),
            pltpu.VMEM((hrows, HEAD_SIZE), F32),
        ],
        compiler_params=params(),
        cost_estimate=cost(10**8, 7 * 10**6),
    )(ctx_len, query, keys, values, token_keys, token_values, received, dst, rows)


def side_by_side(x, near, far, tile=256):
    m, k = x.shape
    n = near.shape[1]
    steps = n // tile

    def kernel(x_ref, near_ref, far_ref, out_ref):
        step = pl.program_id(0)

        @pl.when(step < steps)
        def _():
            out_ref[...] = jnp.dot(x_ref[...], near_ref[...], preferred_element_type=F32).astype(BF)

        @pl.when(step >= steps)
        def _():
            out_ref[...] = jnp.dot(x_ref[...], far_ref[...], preferred_element_type=F32).astype(BF)

    return pl.pallas_call(
        kernel,
        grid=(2 * steps,),
        out_shape=jax.ShapeDtypeStruct((m, 2 * n), BF),
        in_specs=[
            whole(x.shape),
            pl.BlockSpec((k, tile), lambda j: (0, jnp.minimum(j, steps - 1))),
            pl.BlockSpec((k, tile), lambda j: (0, jnp.maximum(j - steps, 0))),
        ],
        out_specs=pl.BlockSpec((m, tile), lambda j: (0, j)),
        compiler_params=params(),
        cost_estimate=cost(4 * m * n * k, 4 * (m * k + k * n)),
    )(x, near, far)


def gate_up(blocks, gains, gates, ups, tile=256):
    count = len(blocks)
    rows, width = blocks[0].shape
    part = width // len(gates)
    hidden = gates[0].shape[1]
    steps = hidden // tile
    full = 2 * hidden + 128

    def kernel(*refs):
        block_refs = refs[:count]
        gain_refs = refs[count : count + 2]
        gate_refs = refs[count + 2 : count + 4]
        up_refs = refs[count + 4 : count + 6]
        out_ref, x_ref = refs[count + 6 :]
        step = pl.program_id(0)

        @pl.when(step == 0)
        def _():
            gain = jnp.concatenate([g[...] for g in gain_refs], axis=1)
            lane = lax.broadcasted_iota(jnp.int32, (rows, 128), 1)
            for i, block_ref in enumerate(block_refs):
                block = block_ref[...].astype(F32)
                x_ref[i * rows : (i + 1) * rows, :] = (block * gain).astype(BF)
                square = jnp.sum(block * block, axis=1, keepdims=True)
                high = square.astype(BF).astype(F32)
                middle = (square - high).astype(BF).astype(F32)
                low = square - high - middle
                out_ref[i, :, 2 * hidden :] = jnp.where(
                    lane == 0, high, jnp.where(lane == 1, middle, jnp.where(lane == 2, low, 0.0))
                ).astype(BF)

        for which, weights in enumerate((gate_refs, up_refs)):
            total = sum(
                jnp.dot(
                    x_ref[:, i * part : (i + 1) * part], w[...], preferred_element_type=F32
                )
                for i, w in enumerate(weights)
            )
            start = pl.multiple_of(which * hidden + step * tile, tile)
            out_ref[:, :, pl.ds(start, tile)] = total.astype(BF).reshape(count, rows, tile)

    weight_spec = pl.BlockSpec((part, tile), lambda j: (0, j))
    return pl.pallas_call(
        kernel,
        grid=(steps,),
        out_shape=jax.ShapeDtypeStruct((count, rows, full), BF),
        in_specs=[whole((rows, width))] * count + [whole((1, part))] * 2 + [weight_spec] * 4,
        out_specs=whole((count, rows, full)),
        scratch_shapes=[pltpu.VMEM((count * rows, width), BF)],
        compiler_params=params(),
        cost_estimate=cost(4 * count * rows * width * hidden, 12 * 10**6),
    )(*blocks, *gains, *gates, *ups)


def activate(parts, hidden, tile=256):
    count, rows, full = parts.shape
    steps = hidden // tile

    def kernel(gate_ref, up_ref, square_ref, out_ref, inv_ref):
        @pl.when(pl.program_id(0) == 0)
        def _():
            square = jnp.sum(square_ref[...].astype(F32), axis=(0, 2))[:, None]
            inv_ref[...] = jnp.broadcast_to(
                lax.rsqrt(square / MODEL_WIDTH + epsilon), inv_ref.shape
            )

        inverse = inv_ref[:, 0:1]
        gate = jnp.sum(gate_ref[...].astype(F32), axis=0) * inverse
        up = jnp.sum(up_ref[...].astype(F32), axis=0) * inverse
        value = (gate / (1.0 + jnp.exp(-gate)) * up).astype(BF)
        out_ref[...] = jnp.broadcast_to(value[None], out_ref.shape)

    return pl.pallas_call(
        kernel,
        grid=(steps,),
        out_shape=jax.ShapeDtypeStruct((CHIPS, rows, hidden), BF),
        in_specs=[
            pl.BlockSpec((count, rows, tile), lambda j: (0, 0, j)),
            pl.BlockSpec((count, rows, tile), lambda j: (0, 0, j + steps)),
            pl.BlockSpec((count, rows, 128), lambda j: (0, 0, 2 * hidden // 128)),
        ],
        out_specs=pl.BlockSpec((CHIPS, rows, tile), lambda j: (0, 0, j)),
        scratch_shapes=[pltpu.VMEM((rows, 128), F32)],
        compiler_params=params(),
        cost_estimate=cost(10**6, 6 * 10**6),
    )(parts, parts, parts)


def body(
    query,
    key_store_cache,
    value_store_cache,
    token_keys,
    token_values,
    pooled_block_keys,
    pooled_block_values,
    block_dst,
    block_row,
    ctx_len,
    residual,
    norm_gain,
    output_weight,
    w_gate,
    w_up,
    w_down,
):
    requests = query.shape[0]
    attn_index = lax.axis_index("attn")
    core = attn_index % 2
    ffn_index = lax.axis_index("ffn")
    pools = block_dst.shape[0] // pooled_block_keys.shape[0]
    flat_dst = block_dst[:, 0]

    output_far = swap_core(output_weight)
    first = ffn_index * (2 * requests)
    residual_near = lax.dynamic_slice_in_dim(residual, first + core * requests, requests, 0)
    residual_far = swap_core(
        lax.dynamic_slice_in_dim(residual, first + (1 - core) * requests, requests, 0)
    )
    gain_near = norm_gain.reshape(1, -1)
    gain_far = swap_core(gain_near)
    gate_far, up_far, down_far = swap_core(w_gate), swap_core(w_up), swap_core(w_down)

    sent = place_blocks(flat_dst, pooled_block_keys, pooled_block_values)
    received = lax.all_to_all(sent, "attn", split_axis=0, concat_axis=0, tiled=True)
    attended = attention(
        ctx_len,
        query,
        key_store_cache,
        value_store_cache,
        token_keys,
        token_values,
        received.reshape(-1, received.shape[2]),
        flat_dst.reshape(pools, -1),
        block_row.reshape(pools, -1),
    )
    attended = exchange_chips(attended).reshape(CHIPS * requests, -1)
    head_part = side_by_side(attended, output_weight, output_far).reshape(CHIPS, requests, -1)
    attn_out = z_scatter_sum(
        lambda d: lax.dynamic_index_in_dim(head_part, (ffn_index + d) % 8, 0, keepdims=False)
    )
    mixed = jnp.concatenate([residual_near, residual_far], axis=1).astype(F32) + attn_out
    blocks = z_gather(mixed.astype(BF))
    parts = gate_up(blocks, (gain_near, gain_far), (w_gate, gate_far), (w_up, up_far))
    activated = activate(exchange_chips(parts), w_gate.shape[1])
    activated = exchange_chips(activated).reshape(CHIPS * requests, -1)
    down_part = side_by_side(activated, w_down, down_far).reshape(CHIPS, requests, -1)
    ffn_out = z_scatter_sum(lambda d: down_part[d % 8])
    layer_out = (mixed + ffn_out).astype(BF)
    half = layer_out.shape[1] // 2
    near = layer_out[:, :half]
    far = swap_core(layer_out[:, half:])
    return jnp.where(
        core == 0, jnp.concatenate([near, far], axis=0), jnp.concatenate([far, near], axis=0)
    )


def solution(mesh):
    placed = (
        P(("grp", "attn"), "ffn"),
        P(("grp", "attn"), None, "ffn"),
        P(("grp", "attn"), None, "ffn"),
        P(("grp", "attn"), "ffn"),
        P(("grp", "attn"), "ffn"),
        P(("grp", "attn"), None, "ffn"),
        P(("grp", "attn"), None, "ffn"),
        P("grp", None),
        P("grp"),
        P(("grp", "attn")),
        P("grp", "attn"),
        P("attn"),
        P("ffn", "attn"),
        P("attn", "ffn"),
        P("attn", "ffn"),
        P("ffn", "attn"),
    )
    return jax.shard_map(
        body, mesh=mesh, in_specs=placed, out_specs=P(("grp", "ffn"), "attn"), check_vma=False
    )
```

time: 379 us -> 238 us (0.63)
  waiting for transfers between devices: 267 us -> 130 us
  starting transfers between devices: 11.8 us -> 59.4 us
  matrix products: 32.3 us -> 0 us
  Pallas kernels: 0 us -> 29.8 us
  blocking collectives: 23.6 us -> 0 us
  other arithmetic: 23.7 us -> 2.55 us
  between operations: 13.3 us -> 0.26 us
  local copies, waits for them, and re-layouts: 6.4 us -> 13.3 us
    reduce_scatter x2 -> x0, waiting for transfers between devices: 109 us -> none  [the longest x1 70.3 us: body(): lax.psum_scatter(jnp.concatenate([jnp.dot(normed, w_gate, preferred_eleme...]
    all_to_all x2 -> x4, waiting for transfers between devices: 0.01 us -> 82 us  [the longest x3 78.7 us: exchange_chips(): lax.all_to_all(value, 'attn', split_axis=0, concat_axis=0, axis_index_gro...]
    all_gather x2 -> x0, waiting for transfers between devices: 80.8 us -> none  [the longest x1 42 us: body(): lax.all_gather(activated, 'attn', axis=0, tiled=True)]
    psum x1 -> x0, waiting for transfers between devices: 76.5 us -> none  [body(): lax.psum(head_part.astype(jnp.bfloat16), 'ffn').astype(jnp.float32)]
    ppermute x0 -> x28, waiting for transfers between devices: none -> 48.1 us  [the longest x21 44.4 us: z_shift(): return lax.ppermute(value, 'ffn', [(f, (f + step) % 8) for f in range(8)])]
    ppermute x0 -> x28, starting transfers between devices: none -> 37.8 us  [the longest x21 36.9 us: z_shift(): return lax.ppermute(value, 'ffn', [(f, (f + step) % 8) for f in range(8)])]
    dot_general x11 -> x0, matrix products: 32.3 us -> none  [the longest x1 6.41 us: body(): jnp.dot(normed, w_up, preferred_element_type=jnp.float32)]
    pallas_call x0 -> x6, Pallas kernels: none -> 29.8 us  [the longest x2 8.31 us: side_by_side(): pl.pallas_call(kernel, grid=(2 * steps,), out_shape=jax.ShapeDtypeStruct(...]
  transfers between devices with their start and end apart: 7 -> 32, of which waited for: 5 -> 20; matrix products, arithmetic and copies ran while one was open for 6% -> 2% of each run, Pallas kernels for 0% -> 5%
where the time goes in v1:
time: 238 us; the launch traced here: 235 us
  waiting for transfers between devices  130 us (55%)
  starting transfers between devices  59.4 us (25%)
  Pallas kernels  29.8 us (13%)
  local copies, waits for them, and re-layouts  13.3 us (6%)
  other arithmetic  2.55 us (1%)
    all_to_all x3, waiting for transfers between devices, exchange_chips(): lax.all_to_all(value, 'attn', split_axis=0, concat_axis=0, axis_index_gro...  78.7 us
    ppermute x21, waiting for transfers between devices, z_shift(): return lax.ppermute(value, 'ffn', [(f, (f + step) % 8) for f in range(8)])  44.4 us
    ppermute x21, starting transfers between devices, z_shift(): return lax.ppermute(value, 'ffn', [(f, (f + step) % 8) for f in range(8)])  36.9 us
    all_to_all x3, starting transfers between devices, exchange_chips(): lax.all_to_all(value, 'attn', split_axis=0, concat_axis=0, axis_index_gro...  15.7 us
    unnamed x25, local copies, waits for them, and re-layouts  11.5 us
    pallas_call x2, Pallas kernels, side_by_side(): pl.pallas_call(kernel, grid=(2 * steps,), out_shape=jax.ShapeDtypeStruct(...  8.31 us
    pallas_call x1, Pallas kernels, gate_up(): pl.pallas_call(kernel, grid=(steps,), out_shape=jax.ShapeDtypeStruct((cou...  7.87 us
    pallas_call x1, Pallas kernels, attention(): pl.pallas_call(kernel, grid=(requests // step_rows,), out_shape=jax.Shape...  6.31 us
  transfers between devices with their start and end apart: 32, of which 20 were waited for; matrix products, arithmetic and copies ran while one was open for 2% of the time, Pallas kernels for 5%

profile of v1, /device:TPU:2, one launch (start us, length us, event | category | flops | bytes accessed | tf_op | source)
XLA Modules:
  0.0 235.4 jit_solution(10412018119602259155)
XLA Ops:
  3.8 5.9 %all-to-all-start = ((bf16[32,16,256]{2,1,0:T(8,128)(2,1)}), bf16[32,16,256]{2,1,0:T(8,128)(2,1)S(1)}, u32[]{:S(2)}, u32[]{:S(2)}) async-start(bf16[32,16,256]{2,1,0:T(8,128)(2,1)} %shard_map.154), calls=%async_computation | async-start | bytes 524288 | tf_op jit(solution)/shard_map/all_to_all | solution.py:385
  11.8 3.3 %all-to-all-done = bf16[32,16,256]{2,1,0:T(8,128)(2,1)S(1)} async-done(((bf16[32,16,256]{2,1,0:T(8,128)(2,1)}), bf16[32,16,256]{2,1,0:T(8,128)(2,1)S(1)}, u32[]{:S(2)}, u32[]{:S(2)}) %all-to-all-start) | async-done | bytes 262176 | tf_op jit(solution)/shard_map/all_to_all | solution.py:385
  21.9 6.3 %shard_map.155 = bf16[8,64,1024]{2,1,0:T(8,128)(2,1)} custom-call(s32[64]{0:T(128)S(1)} %copy-done.10, bf16[64,1024]{1,0:T(8,128)(2,1)S(1)} %copy-done.4, bf16[64,192,128]{2,1,0:T(8,128)(2,1)S(1)} %copy-done.1, bf16[64,192,128]{2,1,0:T(8,128)(2,1)S(1)} %copy-done.2, bf16[64,128]{1,0:T(8,128)(2,1)S(1)} %copy-done.7, bf16[64,128]{1,0:T(8,128)(2,1)S(1)} %copy-done.8, ...), custom_call_target="tpu_custom_call" | custom-call | flops 100000000 | bytes 7000000 | tf_op jit(solution)/shard_map/pallas_call | solution.py:202
  28.2 6.1 %all-to-all-start.1 = ((bf16[8,64,1024]{2,1,0:T(8,128)(2,1)}), bf16[8,64,1024]{2,1,0:T(8,128)(2,1)S(1)}, u32[]{:S(2)}, u32[]{:S(2)}) async-start(bf16[8,64,1024]{2,1,0:T(8,128)(2,1)} %shard_map.155), calls=%async_computation.1 | async-start | bytes 2097152 | tf_op jit(solution)/shard_map/all_to_all | solution.py:38
  34.3 14.7 %all-to-all-done.1 = bf16[8,64,1024]{2,1,0:T(8,128)(2,1)S(1)} async-done(((bf16[8,64,1024]{2,1,0:T(8,128)(2,1)}), bf16[8,64,1024]{2,1,0:T(8,128)(2,1)S(1)}, u32[]{:S(2)}, u32[]{:S(2)}) %all-to-all-start.1) | async-done | bytes 1048608 | tf_op jit(solution)/shard_map/all_to_all | solution.py:38
  49.0 3.6 %shard_map.156 = bf16[512,1024]{1,0:T(8,128)(2,1)S(1)} custom-call(bf16[512,1024]{1,0:T(8,128)(2,1)S(1)} %bitcast.39, bf16[1024,512]{1,0:T(8,128)(2,1)S(1)} %copy-done.3, bf16[1024,512]{1,0:T(8,128)(2,1)} %collective-permute-done.1.far_ref), custom_call_target="tpu_custom_call" | custom-call | flops 1073741824 | bytes 4194304 | tf_op jit(solution)/shard_map/pallas_call | solution.py:246
  55.2 4.0 %collective-permute-start.6 = (bf16[64,1024]{1,0:T(8,128)(2,1)S(1)}, bf16[64,1024]{1,0:T(8,128)(2,1)S(1)}, u32[]{:S(2)}, u32[]{:S(2)}) collective-permute-start(bf16[64,1024]{1,0:T(8,128)(2,1)S(1)} %get-tuple-element.18), channel_id=1, source_target_pairs={{0,14},{2,0},{4,2},{6,4},{8,6},{10,8},{12,10},{14,12},{1,15},{3,1}... | collective-permute-start | bytes 393224 | tf_op jit(solution)/shard_map/ppermute | solution.py:44
  62.2 5.6 %collective-permute-done.3 = bf16[64,1024]{1,0:T(8,128)(2,1)S(1)} collective-permute-done((bf16[64,1024]{1,0:T(8,128)(2,1)S(1)}, bf16[64,1024]{1,0:T(8,128)(2,1)S(1)}, u32[]{:S(2)}, u32[]{:S(2)}) %collective-permute-start.3) | collective-permute-done | bytes 131104 | tf_op jit(solution)/shard_map/ppermute | solution.py:44
  68.0 3.2 %collective-permute-start.7 = (bf16[64,1024]{1,0:T(8,128)(2,1)S(1)}, bf16[64,1024]{1,0:T(8,128)(2,1)S(1)}, u32[]{:S(2)}, u32[]{:S(2)}) collective-permute-start(bf16[64,1024]{1,0:T(8,128)(2,1)S(1)} %get-tuple-element.16), channel_id=1, source_target_pairs={{0,14},{2,0},{4,2},{6,4},{8,6},{10,8},{12,10},{14,12},{1,15},{3,1}... | collective-permute-start | bytes 393224 | tf_op jit(solution)/shard_map/ppermute | solution.py:44
  71.2 2.9 %collective-permute-done.4 = bf16[64,1024]{1,0:T(8,128)(2,1)S(1)} collective-permute-done((bf16[64,1024]{1,0:T(8,128)(2,1)S(1)}, bf16[64,1024]{1,0:T(8,128)(2,1)S(1)}, u32[]{:S(2)}, u32[]{:S(2)}) %collective-permute-start.4) | collective-permute-done | bytes 131104 | tf_op jit(solution)/shard_map/ppermute | solution.py:44
  74.9 3.3 %collective-permute-start.8 = (bf16[64,1024]{1,0:T(8,128)(2,1)S(1)}, bf16[64,1024]{1,0:T(8,128)(2,1)S(1)}, u32[]{:S(2)}, u32[]{:S(2)}) collective-permute-start(bf16[64,1024]{1,0:T(8,128)(2,1)S(1)} %get-tuple-element.14), channel_id=1, source_target_pairs={{0,14},{2,0},{4,2},{6,4},{8,6},{10,8},{12,10},{14,12},{1,15},{3,1}... | collective-permute-start | bytes 393224 | tf_op jit(solution)/shard_map/ppermute | solution.py:44
  81.4 3.2 %collective-permute-start.12 = (bf16[64,1024]{1,0:T(8,128)(2,1)S(1)}, bf16[64,1024]{1,0:T(8,128)(2,1)S(1)}, u32[]{:S(2)}, u32[]{:S(2)}) collective-permute-start(bf16[64,1024]{1,0:T(8,128)(2,1)S(1)} %fusion.6.refs_0_), channel_id=1, source_target_pairs={{0,2},{2,4},{4,6},{6,8},{8,10},{10,12},{12,14},{14,0},{1,3},{3,5},... | collective-permute-start | bytes 393224 | tf_op jit(solution)/shard_map/ppermute | solution.py:44
  84.7 3.4 %collective-permute-done.12.refs_7_ = bf16[64,1024]{1,0:T(8,128)(2,1)S(1)} collective-permute-done((bf16[64,1024]{1,0:T(8,128)(2,1)S(1)}, bf16[64,1024]{1,0:T(8,128)(2,1)S(1)}, u32[]{:S(2)}, u32[]{:S(2)}) %collective-permute-start.12) | collective-permute-done | bytes 131104 | tf_op jit(solution)/shard_map/ppermute | solution.py:44
  88.1 2.5 %collective-permute-start.13 = (bf16[64,1024]{1,0:T(8,128)(2,1)S(1)}, bf16[64,1024]{1,0:T(8,128)(2,1)S(1)}, u32[]{:S(2)}, u32[]{:S(2)}) collective-permute-start(bf16[64,1024]{1,0:T(8,128)(2,1)S(1)} %collective-permute-done.12.refs_7_), channel_id=1, source_target_pairs={{0,2},{2,4},{4,6},{6,8},{8,10},{10,12},{12,14},{14,0},{1,3},{3,5},... | collective-permute-start | bytes 393224 | tf_op jit(solution)/shard_map/ppermute | solution.py:44
  91.4 2.9 %collective-permute-done.13.refs_6_ = bf16[64,1024]{1,0:T(8,128)(2,1)S(1)} collective-permute-done((bf16[64,1024]{1,0:T(8,128)(2,1)S(1)}, bf16[64,1024]{1,0:T(8,128)(2,1)S(1)}, u32[]{:S(2)}, u32[]{:S(2)}) %collective-permute-start.13) | collective-permute-done | bytes 131104 | tf_op jit(solution)/shard_map/ppermute | solution.py:44
  97.6 3.9 %collective-permute-done.14.refs_5_ = bf16[64,1024]{1,0:T(8,128)(2,1)S(1)} collective-permute-done((bf16[64,1024]{1,0:T(8,128)(2,1)S(1)}, bf16[64,1024]{1,0:T(8,128)(2,1)S(1)}, u32[]{:S(2)}, u32[]{:S(2)}) %collective-permute-start.14) | collective-permute-done | bytes 131104 | tf_op jit(solution)/shard_map/ppermute | solution.py:44
  102.8 4.8 %collective-permute-done.15.refs_4_ = bf16[64,1024]{1,0:T(8,128)(2,1)S(1)} collective-permute-done((bf16[64,1024]{1,0:T(8,128)(2,1)S(1)}, bf16[64,1024]{1,0:T(8,128)(2,1)S(1)}, u32[]{:S(2)}, u32[]{:S(2)}) %collective-permute-start.15) | collective-permute-done | bytes 131104 | tf_op jit(solution)/shard_map/ppermute | solution.py:44
  107.6 7.9 %shard_map.157 = bf16[8,64,3712]{2,1,0:T(8,128)(2,1)S(1)} custom-call(bf16[64,1024]{1,0:T(8,128)(2,1)S(1)} %fusion.6.refs_0_, bf16[64,1024]{1,0:T(8,128)(2,1)S(1)} %collective-permute-done.9.refs_1_, bf16[64,1024]{1,0:T(8,128)(2,1)S(1)} %collective-permute-done.10.refs_2_, bf16[64,1024]{1,0:T(8,128)(2,1)S(1)} %collective-permute-done.11.refs_3_, ...), custom_call_target="tpu_custom_call" | custom-call | flops 3758096384 | bytes 12000000 | tf_op jit(solution)/shard_map/pallas_call | solution.py:303
  117.3 4.9 %all-to-all-start.2 = ((bf16[8,64,3712]{2,1,0:T(8,128)(2,1)}), bf16[8,64,3712]{2,1,0:T(8,128)(2,1)}, u32[]{:S(2)}, u32[]{:S(2)}) async-start(bf16[8,64,3712]{2,1,0:T(8,128)(2,1)} %copy-done), calls=%async_computation.2 | async-start | bytes 7602176 | tf_op jit(solution)/shard_map/all_to_all | solution.py:38
  122.3 40.9 %all-to-all-done.2.gate_ref.up_ref.square_ref = bf16[8,64,3712]{2,1,0:T(8,128)(2,1)} async-done(((bf16[8,64,3712]{2,1,0:T(8,128)(2,1)}), bf16[8,64,3712]{2,1,0:T(8,128)(2,1)}, u32[]{:S(2)}, u32[]{:S(2)}) %all-to-all-start.2) | async-done | bytes 3801120 | tf_op jit(solution)/shard_map/all_to_all | solution.py:38
  163.2 5.9 %shard_map.158 = bf16[8,64,1792]{2,1,0:T(8,128)(2,1)} custom-call(bf16[8,64,3712]{2,1,0:T(8,128)(2,1)} %all-to-all-done.2.gate_ref.up_ref.square_ref, bf16[8,64,3712]{2,1,0:T(8,128)(2,1)} %all-to-all-done.2.gate_ref.up_ref.square_ref, bf16[8,64,3712]{2,1,0:T(8,128)(2,1)} %all-to-all-done.2.gate_ref.up_ref.square_ref), custom_call_target="tpu_custom_call" | custom-call | flops 1000000 | bytes 6000000 | tf_op jit(solution)/shard_map/pallas_call | solution.py:333
  169.1 4.7 %all-to-all-start.3 = ((bf16[8,64,1792]{2,1,0:T(8,128)(2,1)}), bf16[8,64,1792]{2,1,0:T(8,128)(2,1)S(1)}, u32[]{:S(2)}, u32[]{:S(2)}) async-start(bf16[8,64,1792]{2,1,0:T(8,128)(2,1)} %shard_map.158), calls=%async_computation.3 | async-start | bytes 3670016 | tf_op jit(solution)/shard_map/all_to_all | solution.py:38
  173.8 23.1 %all-to-all-done.3 = bf16[8,64,1792]{2,1,0:T(8,128)(2,1)S(1)} async-done(((bf16[8,64,1792]{2,1,0:T(8,128)(2,1)}), bf16[8,64,1792]{2,1,0:T(8,128)(2,1)S(1)}, u32[]{:S(2)}, u32[]{:S(2)}) %all-to-all-start.3) | async-done | bytes 1835040 | tf_op jit(solution)/shard_map/all_to_all | solution.py:38
  196.9 4.7 %shard_map.159 = bf16[512,1024]{1,0:T(8,128)(2,1)S(1)} custom-call(bf16[512,1792]{1,0:T(8,128)(2,1)S(1)} %bitcast.40, bf16[1792,512]{1,0:T(8,128)(2,1)} %near_ref.3, bf16[1792,512]{1,0:T(8,128)(2,1)} %collective-permute-done.19.far_ref), custom_call_target="tpu_custom_call" | custom-call | flops 1879048192 | bytes 7340032 | tf_op jit(solution)/shard_map/pallas_call | solution.py:246
  201.7 2.4 %collective-permute-start.20 = (bf16[64,1024]{1,0:T(8,128)(2,1)S(1)}, bf16[64,1024]{1,0:T(8,128)(2,1)S(1)}, u32[]{:S(2)}, u32[]{:S(2)}) collective-permute-start(bf16[64,1024]{1,0:T(8,128)(2,1)S(1)} %get-tuple-element.9), channel_id=1, source_target_pairs={{0,2},{2,4},{4,6},{6,8},{8,10},{10,12},{12,14},{14,0},{1,3},{3,5},... | collective-permute-start | bytes 393224 | tf_op jit(solution)/shard_map/ppermute | solution.py:44
  204.1 5.1 %collective-permute-start.24 = (bf16[64,1024]{1,0:T(8,128)(2,1)S(1)}, bf16[64,1024]{1,0:T(8,128)(2,1)S(1)}, u32[]{:S(2)}, u32[]{:S(2)}) collective-permute-start(bf16[64,1024]{1,0:T(8,128)(2,1)S(1)} %get-tuple-element.10), channel_id=1, source_target_pairs={{0,14},{2,0},{4,2},{6,4},{8,6},{10,8},{12,10},{14,12},{1,15},{3,1}... | collective-permute-start | bytes 393224 | tf_op jit(solution)/shard_map/ppermute | solution.py:44
  209.2 3.1 %collective-permute-done.20 = bf16[64,1024]{1,0:T(8,128)(2,1)S(1)} collective-permute-done((bf16[64,1024]{1,0:T(8,128)(2,1)S(1)}, bf16[64,1024]{1,0:T(8,128)(2,1)S(1)}, u32[]{:S(2)}, u32[]{:S(2)}) %collective-permute-start.20) | collective-permute-done | bytes 131104 | tf_op jit(solution)/shard_map/ppermute | solution.py:44
  212.5 7.5 %collective-permute-done.21 = bf16[64,1024]{1,0:T(8,128)(2,1)S(1)} collective-permute-done((bf16[64,1024]{1,0:T(8,128)(2,1)S(1)}, bf16[64,1024]{1,0:T(8,128)(2,1)S(1)}, u32[]{:S(2)}, u32[]{:S(2)}) %collective-permute-start.21) | collective-permute-done | bytes 131104 | tf_op jit(solution)/shard_map/ppermute | solution.py:44
  220.1 3.2 %collective-permute-start.25 = (bf16[64,1024]{1,0:T(8,128)(2,1)S(1)}, bf16[64,1024]{1,0:T(8,128)(2,1)S(1)}, u32[]{:S(2)}, u32[]{:S(2)}) collective-permute-start(bf16[64,1024]{1,0:T(8,128)(2,1)S(1)} %get-tuple-element.8), channel_id=1, source_target_pairs={{0,14},{2,0},{4,2},{6,4},{8,6},{10,8},{12,10},{14,12},{1,15},{3,1}... | collective-permute-start | bytes 393224 | tf_op jit(solution)/shard_map/ppermute | solution.py:44
  223.4 3.5 %collective-permute-done.22 = bf16[64,1024]{1,0:T(8,128)(2,1)S(1)} collective-permute-done((bf16[64,1024]{1,0:T(8,128)(2,1)S(1)}, bf16[64,1024]{1,0:T(8,128)(2,1)S(1)}, u32[]{:S(2)}, u32[]{:S(2)}) %collective-permute-start.22) | collective-permute-done | bytes 131104 | tf_op jit(solution)/shard_map/ppermute | solution.py:44
  227.8 2.4 %collective-permute-start.26 = (bf16[64,1024]{1,0:T(8,128)(2,1)S(1)}, bf16[64,1024]{1,0:T(8,128)(2,1)S(1)}, u32[]{:S(2)}, u32[]{:S(2)}) collective-permute-start(bf16[64,1024]{1,0:T(8,128)(2,1)S(1)} %get-tuple-element.6), channel_id=1, source_target_pairs={{0,14},{2,0},{4,2},{6,4},{8,6},{10,8},{12,10},{14,12},{1,15},{3,1}... | collective-permute-start | bytes 393224 | tf_op jit(solution)/shard_map/ppermute | solution.py:44
  230.3 2.9 %collective-permute-done.23 = bf16[64,1024]{1,0:T(8,128)(2,1)S(1)} collective-permute-done((bf16[64,1024]{1,0:T(8,128)(2,1)S(1)}, bf16[64,1024]{1,0:T(8,128)(2,1)S(1)}, u32[]{:S(2)}, u32[]{:S(2)}) %collective-permute-start.23) | collective-permute-done | bytes 131104 | tf_op jit(solution)/shard_map/ppermute | solution.py:44
  (79 shorter events, 33.0 us)
Async XLA Ops:
  3.8 11.3 %all-to-all-start = ((bf16[32,16,256]{2,1,0:T(8,128)(2,1)}), bf16[32,16,256]{2,1,0:T(8,128)(2,1)S(1)}, u32[]{:S(2)}, u32[]{:S(2)}) async-start(bf16[32,16,256]{2,1,0:T(8,128)(2,1)} %shard_map.154), calls=%async_computation | async-start | bytes 524288 | tf_op jit(solution)/shard_map/all_to_all | solution.py:385
  9.6 24.7 %collective-permute-start.1 = (bf16[1024,512]{1,0:T(8,128)(2,1)}, bf16[1024,512]{1,0:T(8,128)(2,1)}, u32[]{:S(2)}, u32[]{:S(2)}) collective-permute-start(bf16[1024,512]{1,0:T(8,128)(2,1)} %near_ref.2), channel_id=1, source_target_pairs={{0,16},{16,0},{32,48},{48,32},{64,80},{80,64},{96,112},{112,96},{1... | collective-permute-start | bytes 3145736 | tf_op jit(solution)/shard_map/ppermute | solution.py:33
  28.2 20.8 %all-to-all-start.1 = ((bf16[8,64,1024]{2,1,0:T(8,128)(2,1)}), bf16[8,64,1024]{2,1,0:T(8,128)(2,1)S(1)}, u32[]{:S(2)}, u32[]{:S(2)}) async-start(bf16[8,64,1024]{2,1,0:T(8,128)(2,1)} %shard_map.155), calls=%async_computation.1 | async-start | bytes 2097152 | tf_op jit(solution)/shard_map/all_to_all | solution.py:38
  52.7 8.9 %collective-permute-start.2 = (bf16[64,1024]{1,0:T(8,128)(2,1)S(1)}, bf16[64,1024]{1,0:T(8,128)(2,1)S(1)}, u32[]{:S(2)}, u32[]{:S(2)}) collective-permute-start(bf16[64,1024]{1,0:T(8,128)(2,1)S(1)} %get-tuple-element.17), channel_id=1, source_target_pairs={{0,2},{2,4},{4,6},{6,8},{8,10},{10,12},{12,14},{14,0},{1,3},{3,5},... | collective-permute-start | bytes 393224 | tf_op jit(solution)/shard_map/ppermute | solution.py:44
  54.7 48.1 %collective-permute-start.17 = (bf16[512,1792]{1,0:T(8,128)(2,1)}, bf16[512,1792]{1,0:T(8,128)(2,1)S(1)}, u32[]{:S(2)}, u32[]{:S(2)}) collective-permute-start(bf16[512,1792]{1,0:T(8,128)(2,1)} %refs_10_.1), channel_id=1, source_target_pairs={{0,16},{16,0},{32,48},{48,32},{64,80},{80,64},{96,112},{112,96},{1... | collective-permute-start | bytes 5505032 | tf_op jit(solution)/shard_map/ppermute | solution.py:33
  54.7 48.1 %collective-permute-start.18 = (bf16[512,1792]{1,0:T(8,128)(2,1)}, bf16[512,1792]{1,0:T(8,128)(2,1)}, u32[]{:S(2)}, u32[]{:S(2)}) collective-permute-start(bf16[512,1792]{1,0:T(8,128)(2,1)} %refs_12_.1), channel_id=1, source_target_pairs={{0,16},{16,0},{32,48},{48,32},{64,80},{80,64},{96,112},{112,96},{1... | collective-permute-start | bytes 5505032 | tf_op jit(solution)/shard_map/ppermute | solution.py:33
  55.2 7.1 %collective-permute-start.6 = (bf16[64,1024]{1,0:T(8,128)(2,1)S(1)}, bf16[64,1024]{1,0:T(8,128)(2,1)S(1)}, u32[]{:S(2)}, u32[]{:S(2)}) collective-permute-start(bf16[64,1024]{1,0:T(8,128)(2,1)S(1)} %get-tuple-element.18), channel_id=1, source_target_pairs={{0,14},{2,0},{4,2},{6,4},{8,6},{10,8},{12,10},{14,12},{1,15},{3,1}... | collective-permute-start | bytes 393224 | tf_op jit(solution)/shard_map/ppermute | solution.py:44
  61.6 6.3 %collective-permute-start.3 = (bf16[64,1024]{1,0:T(8,128)(2,1)S(1)}, bf16[64,1024]{1,0:T(8,128)(2,1)S(1)}, u32[]{:S(2)}, u32[]{:S(2)}) collective-permute-start(bf16[64,1024]{1,0:T(8,128)(2,1)S(1)} %fusion.5), channel_id=1, source_target_pairs={{0,2},{2,4},{4,6},{6,8},{8,10},{10,12},{12,14},{14,0},{1,3},{3,5},... | collective-permute-start | bytes 393224 | tf_op jit(solution)/shard_map/ppermute | solution.py:44
  67.9 6.3 %collective-permute-start.4 = (bf16[64,1024]{1,0:T(8,128)(2,1)S(1)}, bf16[64,1024]{1,0:T(8,128)(2,1)S(1)}, u32[]{:S(2)}, u32[]{:S(2)}) collective-permute-start(bf16[64,1024]{1,0:T(8,128)(2,1)S(1)} %get-tuple-element.15), channel_id=1, source_target_pairs={{0,2},{2,4},{4,6},{6,8},{8,10},{10,12},{12,14},{14,0},{1,3},{3,5},... | collective-permute-start | bytes 393224 | tf_op jit(solution)/shard_map/ppermute | solution.py:44
  68.0 6.2 %collective-permute-start.7 = (bf16[64,1024]{1,0:T(8,128)(2,1)S(1)}, bf16[64,1024]{1,0:T(8,128)(2,1)S(1)}, u32[]{:S(2)}, u32[]{:S(2)}) collective-permute-start(bf16[64,1024]{1,0:T(8,128)(2,1)S(1)} %get-tuple-element.16), channel_id=1, source_target_pairs={{0,14},{2,0},{4,2},{6,4},{8,6},{10,8},{12,10},{14,12},{1,15},{3,1}... | collective-permute-start | bytes 393224 | tf_op jit(solution)/shard_map/ppermute | solution.py:44
  74.9 6.4 %collective-permute-start.5 = (bf16[64,1024]{1,0:T(8,128)(2,1)}, bf16[64,1024]{1,0:T(8,128)(2,1)S(1)}, u32[]{:S(2)}, u32[]{:S(2)}) collective-permute-start(bf16[64,1024]{1,0:T(8,128)(2,1)} %get-tuple-element.13), channel_id=1, source_target_pairs={{0,2},{2,4},{4,6},{6,8},{8,10},{10,12},{12,14},{14,0},{1,3},{3,5},... | collective-permute-start | bytes 393224 | tf_op jit(solution)/shard_map/ppermute | solution.py:44
  74.9 6.4 %collective-permute-start.8 = (bf16[64,1024]{1,0:T(8,128)(2,1)S(1)}, bf16[64,1024]{1,0:T(8,128)(2,1)S(1)}, u32[]{:S(2)}, u32[]{:S(2)}) collective-permute-start(bf16[64,1024]{1,0:T(8,128)(2,1)S(1)} %get-tuple-element.14), channel_id=1, source_target_pairs={{0,14},{2,0},{4,2},{6,4},{8,6},{10,8},{12,10},{14,12},{1,15},{3,1}... | collective-permute-start | bytes 393224 | tf_op jit(solution)/shard_map/ppermute | solution.py:44
  79.1 1.3 collective-permute-start
  81.4 6.7 %collective-permute-start.12 = (bf16[64,1024]{1,0:T(8,128)(2,1)S(1)}, bf16[64,1024]{1,0:T(8,128)(2,1)S(1)}, u32[]{:S(2)}, u32[]{:S(2)}) collective-permute-start(bf16[64,1024]{1,0:T(8,128)(2,1)S(1)} %fusion.6.refs_0_), channel_id=1, source_target_pairs={{0,2},{2,4},{4,6},{6,8},{8,10},{10,12},{12,14},{14,0},{1,3},{3,5},... | collective-permute-start | bytes 393224 | tf_op jit(solution)/shard_map/ppermute | solution.py:44
  84.6 6.0 %collective-permute-start.9 = (bf16[64,1024]{1,0:T(8,128)(2,1)S(1)}, bf16[64,1024]{1,0:T(8,128)(2,1)S(1)}, u32[]{:S(2)}, u32[]{:S(2)}) collective-permute-start(bf16[64,1024]{1,0:T(8,128)(2,1)S(1)} %fusion.6.refs_0_), channel_id=1, source_target_pairs={{0,14},{2,0},{4,2},{6,4},{8,6},{10,8},{12,10},{14,12},{1,15},{3,1}... | collective-permute-start | bytes 393224 | tf_op jit(solution)/shard_map/ppermute | solution.py:44
  88.1 6.2 %collective-permute-start.13 = (bf16[64,1024]{1,0:T(8,128)(2,1)S(1)}, bf16[64,1024]{1,0:T(8,128)(2,1)S(1)}, u32[]{:S(2)}, u32[]{:S(2)}) collective-permute-start(bf16[64,1024]{1,0:T(8,128)(2,1)S(1)} %collective-permute-done.12.refs_7_), channel_id=1, source_target_pairs={{0,2},{2,4},{4,6},{6,8},{8,10},{10,12},{12,14},{14,0},{1,3},{3,5},... | collective-permute-start | bytes 393224 | tf_op jit(solution)/shard_map/ppermute | solution.py:44
  90.6 5.9 %collective-permute-start.10 = (bf16[64,1024]{1,0:T(8,128)(2,1)S(1)}, bf16[64,1024]{1,0:T(8,128)(2,1)S(1)}, u32[]{:S(2)}, u32[]{:S(2)}) collective-permute-start(bf16[64,1024]{1,0:T(8,128)(2,1)S(1)} %collective-permute-done.9.refs_1_), channel_id=1, source_target_pairs={{0,14},{2,0},{4,2},{6,4},{8,6},{10,8},{12,10},{14,12},{1,15},{3,1}... | collective-permute-start | bytes 393224 | tf_op jit(solution)/shard_map/ppermute | solution.py:44
  94.3 7.1 %collective-permute-start.14 = (bf16[64,1024]{1,0:T(8,128)(2,1)S(1)}, bf16[64,1024]{1,0:T(8,128)(2,1)S(1)}, u32[]{:S(2)}, u32[]{:S(2)}) collective-permute-start(bf16[64,1024]{1,0:T(8,128)(2,1)S(1)} %collective-permute-done.13.refs_6_), channel_id=1, source_target_pairs={{0,2},{2,4},{4,6},{6,8},{8,10},{10,12},{12,14},{14,0},{1,3},{3,5},... | collective-permute-start | bytes 393224 | tf_op jit(solution)/shard_map/ppermute | solution.py:44
  96.5 6.3 %collective-permute-start.11 = (bf16[64,1024]{1,0:T(8,128)(2,1)S(1)}, bf16[64,1024]{1,0:T(8,128)(2,1)S(1)}, u32[]{:S(2)}, u32[]{:S(2)}) collective-permute-start(bf16[64,1024]{1,0:T(8,128)(2,1)S(1)} %collective-permute-done.10.refs_2_), channel_id=1, source_target_pairs={{0,14},{2,0},{4,2},{6,4},{8,6},{10,8},{12,10},{14,12},{1,15},{3,1}... | collective-permute-start | bytes 393224 | tf_op jit(solution)/shard_map/ppermute | solution.py:44
  101.4 6.2 %collective-permute-start.15 = (bf16[64,1024]{1,0:T(8,128)(2,1)S(1)}, bf16[64,1024]{1,0:T(8,128)(2,1)S(1)}, u32[]{:S(2)}, u32[]{:S(2)}) collective-permute-start(bf16[64,1024]{1,0:T(8,128)(2,1)S(1)} %collective-permute-done.14.refs_5_), channel_id=1, source_target_pairs={{0,2},{2,4},{4,6},{6,8},{8,10},{10,12},{12,14},{14,0},{1,3},{3,5},... | collective-permute-start | bytes 393224 | tf_op jit(solution)/shard_map/ppermute | solution.py:44
  101.6 1.2 collective-permute-start.16
  117.3 45.9 %all-to-all-start.2 = ((bf16[8,64,3712]{2,1,0:T(8,128)(2,1)}), bf16[8,64,3712]{2,1,0:T(8,128)(2,1)}, u32[]{:S(2)}, u32[]{:S(2)}) async-start(bf16[8,64,3712]{2,1,0:T(8,128)(2,1)} %copy-done), calls=%async_computation.2 | async-start | bytes 7602176 | tf_op jit(solution)/shard_map/all_to_all | solution.py:38
  122.3 51.5 %collective-permute-start.19 = (bf16[1792,512]{1,0:T(8,128)(2,1)}, bf16[1792,512]{1,0:T(8,128)(2,1)}, u32[]{:S(2)}, u32[]{:S(2)}) collective-permute-start(bf16[1792,512]{1,0:T(8,128)(2,1)} %near_ref.3), channel_id=1, source_target_pairs={{0,16},{16,0},{32,48},{48,32},{64,80},{80,64},{96,112},{112,96},{1... | collective-permute-start | bytes 5505032 | tf_op jit(solution)/shard_map/ppermute | solution.py:33
  169.1 27.8 %all-to-all-start.3 = ((bf16[8,64,1792]{2,1,0:T(8,128)(2,1)}), bf16[8,64,1792]{2,1,0:T(8,128)(2,1)S(1)}, u32[]{:S(2)}, u32[]{:S(2)}) async-start(bf16[8,64,1792]{2,1,0:T(8,128)(2,1)} %shard_map.158), calls=%async_computation.3 | async-start | bytes 3670016 | tf_op jit(solution)/shard_map/all_to_all | solution.py:38
  201.7 10.6 %collective-permute-start.20 = (bf16[64,1024]{1,0:T(8,128)(2,1)S(1)}, bf16[64,1024]{1,0:T(8,128)(2,1)S(1)}, u32[]{:S(2)}, u32[]{:S(2)}) collective-permute-start(bf16[64,1024]{1,0:T(8,128)(2,1)S(1)} %get-tuple-element.9), channel_id=1, source_target_pairs={{0,2},{2,4},{4,6},{6,8},{8,10},{10,12},{12,14},{14,0},{1,3},{3,5},... | collective-permute-start | bytes 393224 | tf_op jit(solution)/shard_map/ppermute | solution.py:44
  204.1 8.4 %collective-permute-start.24 = (bf16[64,1024]{1,0:T(8,128)(2,1)S(1)}, bf16[64,1024]{1,0:T(8,128)(2,1)S(1)}, u32[]{:S(2)}, u32[]{:S(2)}) collective-permute-start(bf16[64,1024]{1,0:T(8,128)(2,1)S(1)} %get-tuple-element.10), channel_id=1, source_target_pairs={{0,14},{2,0},{4,2},{6,4},{8,6},{10,8},{12,10},{14,12},{1,15},{3,1}... | collective-permute-start | bytes 393224 | tf_op jit(solution)/shard_map/ppermute | solution.py:44
  212.4 7.6 %collective-permute-start.21 = (bf16[64,1024]{1,0:T(8,128)(2,1)S(1)}, bf16[64,1024]{1,0:T(8,128)(2,1)S(1)}, u32[]{:S(2)}, u32[]{:S(2)}) collective-permute-start(bf16[64,1024]{1,0:T(8,128)(2,1)S(1)} %add_convert_fusion.5), channel_id=1, source_target_pairs={{0,2},{2,4},{4,6},{6,8},{8,10},{10,12},{12,14},{14,0},{1,3},{3,5},... | collective-permute-start | bytes 393224 | tf_op jit(solution)/shard_map/ppermute | solution.py:44
  220.1 6.8 %collective-permute-start.22 = (bf16[64,1024]{1,0:T(8,128)(2,1)S(1)}, bf16[64,1024]{1,0:T(8,128)(2,1)S(1)}, u32[]{:S(2)}, u32[]{:S(2)}) collective-permute-start(bf16[64,1024]{1,0:T(8,128)(2,1)S(1)} %get-tuple-element.7), channel_id=1, source_target_pairs={{0,2},{2,4},{4,6},{6,8},{8,10},{10,12},{12,14},{14,0},{1,3},{3,5},... | collective-permute-start | bytes 393224 | tf_op jit(solution)/shard_map/ppermute | solution.py:44
  220.1 6.7 %collective-permute-start.25 = (bf16[64,1024]{1,0:T(8,128)(2,1)S(1)}, bf16[64,1024]{1,0:T(8,128)(2,1)S(1)}, u32[]{:S(2)}, u32[]{:S(2)}) collective-permute-start(bf16[64,1024]{1,0:T(8,128)(2,1)S(1)} %get-tuple-element.8), channel_id=1, source_target_pairs={{0,14},{2,0},{4,2},{6,4},{8,6},{10,8},{12,10},{14,12},{1,15},{3,1}... | collective-permute-start | bytes 393224 | tf_op jit(solution)/shard_map/ppermute | solution.py:44
  226.9 6.3 %collective-permute-start.23 = (bf16[64,1024]{1,0:T(8,128)(2,1)S(1)}, bf16[64,1024]{1,0:T(8,128)(2,1)S(1)}, u32[]{:S(2)}, u32[]{:S(2)}) collective-permute-start(bf16[64,1024]{1,0:T(8,128)(2,1)S(1)} %get-tuple-element.5), channel_id=1, source_target_pairs={{0,2},{2,4},{4,6},{6,8},{8,10},{10,12},{12,14},{14,0},{1,3},{3,5},... | collective-permute-start | bytes 393224 | tf_op jit(solution)/shard_map/ppermute | solution.py:44
  227.8 5.4 %collective-permute-start.26 = (bf16[64,1024]{1,0:T(8,128)(2,1)S(1)}, bf16[64,1024]{1,0:T(8,128)(2,1)S(1)}, u32[]{:S(2)}, u32[]{:S(2)}) collective-permute-start(bf16[64,1024]{1,0:T(8,128)(2,1)S(1)} %get-tuple-element.6), channel_id=1, source_target_pairs={{0,14},{2,0},{4,2},{6,4},{8,6},{10,8},{12,10},{14,12},{1,15},{3,1}... | collective-permute-start | bytes 393224 | tf_op jit(solution)/shard_map/ppermute | solution.py:44
  233.4 1.3 collective-permute-start.27
  (12 other events, 80.9 us)
